TPU v7x, 256 devices: a whole 4x4x8 slice. The times are simulated.
256 devices in a mesh: gy: 32 (over z_hi, y, x), gz: 8 (over z_lo, core).
Axes of the slice: x: 4, y: 4, z: 8 (z_hi: 2, z_lo: 4; z = z_hi * 4 + z_lo), core: 2. Of those that a mesh axis runs over, the one named last changes fastest.
Arguments:
- kspace: float32 [2, 4, 256, 32, 256], P(None, None, 'gy', 'gz'), may hold values from -6 to 6
- cotangent: float32 [2, 4, 256, 32, 256], P(None, None, 'gy', 'gz'), may hold values from -6 to 6
- weight_in: bfloat16 [16, 8, 3, 3, 3], replicated, may hold values from -0.4375 to 0.4375
- weight_out: bfloat16 [8, 16, 3, 3, 3], replicated, may hold values from -0.3125 to 0.3125
- consistency_weight: float32 [1], replicated, may hold values from 0.2 to 1
- sampling_mask: int32 [256, 32], P('gy', 'gz'), may hold values 0 or 1
Outputs:
- grad_kspace: float32 [2, 4, 256, 32, 256], P(None, None, 'gy', 'gz')
- grad_weight_in: float32 [16, 8, 3, 3, 3], replicated
- grad_weight_out: float32 [8, 16, 3, 3, 3], replicated
Inputs may be any that keep to these rules, and one draw needn't show every extreme that they name: `sampling_mask`: 1 marks a sampled phase-encode line.
All inputs are finite; a program needn't handle non-finite values. No bound on the sum of `sampling_mask` on one device may be relied on, other than what follows from the above.
Results may differ from a plain program's by a relative error of at most 0.0059.
Values may be sent and summed in bfloat16 or wider, within the bound.
A program may use at most 128 MiB of HBM per device.

v0:
```python
import math
import jax
import jax.numpy as jnp
from jax import lax
from jax.sharding import PartitionSpec as P


def as_sent(shard):
    return jax.tree.map(lambda a: a.astype(jnp.bfloat16) if a.dtype == jnp.float32 else a, shard)


def extended(shard, sides, width):
    for axis, dim in sides:
        count, length = (lax.axis_size(axis), shard.shape[dim])
        up = [(i, (i + 1) % count) for i in range(count - 1)]
        down = [(j, i) for i, j in up]
        last = lax.slice_in_dim(shard, length - width, length, axis=dim)
        first = lax.slice_in_dim(shard, 0, width, axis=dim)
        before = lax.ppermute(last, axis, up)
        after = lax.ppermute(first, axis, down)
        shard = jnp.concatenate([before, shard, after], axis=dim)
    return shard


def dft_table(length, direction):
    indices = lax.iota(jnp.int32, length)
    products = indices[:, None] * indices[None, :] % length
    phases = products.astype(jnp.float32) * (2.0 * math.pi / length)
    cosine = jnp.cos(phases) / math.sqrt(length)
    sine_part = direction * jnp.sin(phases) / math.sqrt(length)
    return jnp.stack([jnp.stack([cosine, -sine_part]), jnp.stack([sine_part, cosine])])


def spectral(spectrum, direction):
    field_parts = spectrum.shape[1]
    cells_y = spectrum.shape[2]
    cells_z = spectrum.shape[3]
    readout = spectrum.shape[4]
    length_y = cells_y * lax.axis_size("gy")
    length_z = cells_z * lax.axis_size("gz")
    table_y = dft_table(length_y, direction)
    table_z = dft_table(length_z, direction)
    flattened = spectrum.reshape(2, field_parts, cells_y, cells_z * readout)
    transformed_y = jnp.einsum(
        "pqvy,qcym->pcvm",
        table_y,
        lax.all_to_all(flattened, "gy", split_axis=3, concat_axis=2, tiled=True),
        precision=lax.Precision.HIGHEST,
    )
    turned_field = lax.all_to_all(
        lax.all_to_all(transformed_y, "gy", split_axis=2, concat_axis=3, tiled=True),
        "gz",
        split_axis=2,
        concat_axis=3,
        tiled=True,
    )
    shaped = turned_field.reshape(
        turned_field.shape[0], turned_field.shape[1], turned_field.shape[2], length_z, readout
    )
    turned = jnp.einsum("pqwz,qcyzx->pcywx", table_z, shaped, precision=lax.Precision.HIGHEST)
    transformed_z = turned.reshape(turned_field.shape)
    result = lax.all_to_all(
        as_sent(transformed_z), "gz", split_axis=3, concat_axis=2, tiled=True
    ).astype(transformed_z.dtype)
    return result.reshape(spectrum.shape)


def with_rims(volume):
    return extended(volume, (("gy", 2), ("gz", 3)), 1)


def convolve(padded, kernel):
    return lax.conv_general_dilated(
        padded,
        kernel,
        (1, 1, 1),
        ((0, 0), (0, 0), (1, 1)),
        dimension_numbers=("NCDHW", "OIDHW", "NCDHW"),
        preferred_element_type=jnp.float32,
    )


def kernel_gradient(padded, cotangent_part):
    summed = lax.conv_general_dilated(
        padded,
        cotangent_part,
        (1, 1, 1),
        ((0, 0), (0, 0), (1, 1)),
        dimension_numbers=("CNDHW", "IODHW", "NCDHW"),
        preferred_element_type=jnp.float32,
    )
    return summed.transpose(1, 0, 2, 3, 4)


def flipped(kernel):
    return jnp.flip(kernel, (2, 3, 4)).transpose(1, 0, 2, 3, 4)


def local(kspace, cotangent, weight_in, weight_out, consistency_weight, sampling_mask):
    coil_count = kspace.shape[1]
    channels = 2 * coil_count
    cells_y = kspace.shape[2]
    cells_z = kspace.shape[3]
    readout = kspace.shape[4]
    voxels = readout * cells_y * cells_z * lax.axis_size("gy") * lax.axis_size("gz")
    image_field = spectral(kspace, 1.0)
    back_field = spectral(cotangent, 1.0)
    image_in = image_field.astype(jnp.bfloat16).reshape(1, channels, cells_y, cells_z, readout)
    back_out = (-back_field).astype(jnp.bfloat16).reshape(1, channels, cells_y, cells_z, readout)
    image_padded = with_rims(image_in)
    back_padded = with_rims(back_out)
    hidden = convolve(image_padded, weight_in)
    active = jax.nn.silu(hidden).astype(jnp.bfloat16)
    active_padded = with_rims(active)
    local_out = kernel_gradient(active_padded, back_out)
    back_active = convolve(back_padded, flipped(weight_out))
    gate = jax.nn.sigmoid(hidden)
    back_hidden = (back_active * gate * (1.0 + hidden * (1.0 - gate))).astype(jnp.bfloat16)
    local_in = kernel_gradient(image_padded, back_hidden)
    hidden_padded = with_rims(back_hidden)
    back_image = convolve(hidden_padded, flipped(weight_in))
    spectrum = spectral(back_image.reshape(2, coil_count, cells_y, cells_z, readout), -1.0)
    summed_in, summed_out = lax.psum((local_in, local_out), ("gy", "gz"))
    scale = 1.0 / math.sqrt(voxels)
    mask_field = sampling_mask.astype(jnp.float32)[None, None, :, :, None]
    grad_kspace = cotangent - consistency_weight[0] * mask_field * cotangent + spectrum
    return (grad_kspace, summed_in * scale, summed_out * scale)


def solution(mesh):
    placed = (
        P(None, None, "gy", "gz", None),
        P(None, None, "gy", "gz", None),
        P(),
        P(),
        P(),
        P("gy", "gz"),
    )
    return jax.shard_map(
        local,
        mesh=mesh,
        in_specs=placed,
        out_specs=(P(None, None, "gy", "gz", None), P(), P()),
        check_vma=False,
    )
```

profile of v0, /device:TPU:1, one launch (start us, length us, event | category | flops | bytes accessed | tf_op | source)
XLA Modules:
  0.0 722.7 jit_solution(2760864033944492216)
XLA Ops:
  0.7 4.5 copy.348
  5.2 6.9 reshape.431
  12.1 14.5 %all-to-all-start.4 = ((f32[32,1,2048]{2,1,0:T(1,128)}), f32[32,1,2048]{2,1,0:T(1,128)S(1)}, u32[]{:S(2)}, u32[]{:S(2)}) async-start(f32[32,1,2048]{2,1,0:T(1,128)} %reshape.431), calls=%async_computation.4 | async-start | bytes 524288 | tf_op jit(solution)/shard_map/all_to_all | solution.py:47
  29.7 6.9 reshape.437
  38.5 11.0 %all-to-all-start = ((f32[32,1,2048]{2,1,0:T(1,128)}), f32[32,1,2048]{2,1,0:T(1,128)S(1)}, u32[]{:S(2)}, u32[]{:S(2)}) async-start(f32[32,1,2048]{2,1,0:T(1,128)} %reshape.437), calls=%async_computation | async-start | bytes 524288 | tf_op jit(solution)/shard_map/all_to_all | solution.py:47
  54.6 6.3 reshape.432
  60.9 3.5 copy.417
  68.4 12.0 %all-to-all-start.5 = ((f32[32,1,2048]{2,1,0:T(1,128)}), f32[32,1,2048]{2,1,0:T(1,128)S(1)}, u32[]{:S(2)}, u32[]{:S(2)}) async-start(f32[32,1,2048]{2,1,0:T(1,128)} %reshape.433), calls=%async_computation.5 | async-start | bytes 524288 | tf_op jit(solution)/shard_map/all_to_all | solution.py:51
  81.7 6.3 reshape.438
  88.0 3.5 copy.411
  95.5 11.8 %all-to-all-start.1 = ((f32[32,1,2048]{2,1,0:T(1,128)}), f32[32,1,2048]{2,1,0:T(1,128)S(1)}, u32[]{:S(2)}, u32[]{:S(2)}) async-start(f32[32,1,2048]{2,1,0:T(1,128)} %reshape.439), calls=%async_computation.1 | async-start | bytes 524288 | tf_op jit(solution)/shard_map/all_to_all | solution.py:51
  110.7 8.5 %all-to-all-done.1 = f32[32,1,2048]{2,1,0:T(1,128)S(1)} async-done(((f32[32,1,2048]{2,1,0:T(1,128)}), f32[32,1,2048]{2,1,0:T(1,128)S(1)}, u32[]{:S(2)}, u32[]{:S(2)}) %all-to-all-start.1) | async-done | bytes 262176 | tf_op jit(solution)/shard_map/all_to_all | solution.py:51
  119.2 7.4 %all-to-all-start.6 = ((f32[2,4,8,1024]{3,1,0,2:T(4,128)}), f32[2,4,8,1024]{3,1,0,2:T(4,128)S(1)}, u32[]{:S(2)}, u32[]{:S(2)}) async-start(f32[2,4,8,1024]{3,1,0,2:T(4,128)} %reshape.424), calls=%async_computation.6 | async-start | bytes 524288 | tf_op jit(solution)/shard_map/all_to_all | solution.py:50
  130.3 5.1 all-to-all-done.6
  135.4 4.8 all-to-all-start.2
  141.7 5.0 copy.421
  146.6 9.3 %reshape.435 = bf16[8,2,4096]{2,1,0:T(2,128)(2,1)} reshape(bf16[8192,1,2,4]{3,2,1,0:T(2,128)(2,1)} %bitcast.299) | data formatting | bytes 262144
  156.0 5.1 all-to-all-start.7
  162.4 5.0 copy.415
  167.4 9.3 %reshape.441 = bf16[8,2,4096]{2,1,0:T(2,128)(2,1)} reshape(bf16[8192,1,2,4]{3,2,1,0:T(2,128)(2,1)} %bitcast.300) | data formatting | bytes 262144
  176.7 5.1 all-to-all-start.3
  182.5 10.0 %reshape.436 = bf16[8192,1,2,4]{3,2,1,0:T(2,128)(2,1)} reshape(bf16[8,2,4096]{2,1,0:T(2,128)(2,1)S(1)} %all-to-all-done.7) | data formatting | bytes 262144
  192.6 8.6 %copy.358 = bf16[2,4,1,8192]{3,1,0,2:T(4,128)(2,1)S(1)} copy(bf16[2,4,1,8192]{1,0,2,3:T(2,128)(2,1)} %bitcast.301) | data formatting | bytes 262144 | tf_op jit(solution)/shard_map/all_to_all | solution.py:62
  203.3 10.1 %reshape.442 = bf16[8192,1,2,4]{3,2,1,0:T(2,128)(2,1)} reshape(bf16[8,2,4096]{2,1,0:T(2,128)(2,1)S(1)} %all-to-all-done.3) | data formatting | bytes 262144
  213.4 8.6 %copy.344 = bf16[2,4,1,8192]{3,1,2,0:T(4,128)(2,1)S(1)} copy(bf16[2,4,1,8192]{1,0,2,3:T(2,128)(2,1)} %bitcast.302) | data formatting | bytes 262144 | tf_op jit(solution)/shard_map/all_to_all | solution.py:62
  222.2 7.4 %copy.396 = bf16[1,8,8,4,256]{1,0,4,3,2:T(2,128)(2,1)} copy(bf16[1,8,8,4,256]{4,3,2,1,0:T(4,128)(2,1)S(1)} %convert_element_type.199) | data formatting | bytes 262144 | tf_op jit(solution)/shard_map/convert_element_type | solution.py:109
  230.9 4.0 collective-permute-start
  236.5 4.4 collective-permute-start.6
  243.7 3.6 collective-permute-start.2
  254.5 4.8 copy.361
  263.3 4.6 copy.347
  269.0 9.1 %multiply_convert_fusion.1 = (bf16[8,4,8,33,16]{4,2,3,1,0:T(8,128)(2,1)}, f32[8,4,8,33,16]{4,2,3,1,0:T(8,128)S(1)}) fusion(pred[8,33]{0,1:T(8,128)(4,1)S(1)} %copy-done.15, bf16[16,8,3,3,3]{0,1,4,3,2:T(8,128)(2,1)S(1)} %copy-done, bf16[8,10,6,1,7,2]{0,4,5,2,1,3:T(8,128)(2,1)S(1)} %copy-done.8, bf16[8,10,6,1,8,33]{0,4,5,2,1,3:T(8,128)(2,1)} %copy.361), kind=kOutput, calls=%fused_computation.16 | convolution fusion | flops 60009984 | bytes 1085064 | tf_op jit(solution)/shard_map/conv_general_dilated | solution.py:73
  278.2 9.5 %multiply_convert_fusion = bf16[8,4,8,33,16]{4,2,3,1,0:T(8,128)(2,1)} fusion(f32[8,4,8,33,16]{4,2,3,1,0:T(8,128)S(1)} %get-tuple-element.36, bf16[8,16,3,3,3]{1,0,4,3,2:T(8,128)(2,1)S(1)} %copy-done.14, bf16[8,10,6,1,7,2]{0,4,5,2,1,3:T(8,128)(2,1)S(1)} %slice.86, bf16[8,10,6,1,8,33]{0,4,5,2,1,3:T(8,128)(2,1)S(1)} %copy-done.2, pred[8,33]{0,1:T(8,128)(4,1)S(1)} %copy-done.15), kind=kOutput, calls=%fused_computation.15 | convolution fusion | flops 60685824 | bytes 1085064 | tf_op jit(solution)/shard_map/conv_general_dilated | solution.py:73
  287.7 3.7 copy.363
  296.9 5.2 collective-permute-start.12
  306.7 4.0 collective-permute-start.8
  312.5 4.8 copy.442
  320.3 4.5 collective-permute-start.10
  326.7 4.0 fusion.33
  330.7 3.5 copy.441
  340.1 4.7 copy.368
  345.9 9.1 %broadcast_select_fusion = f32[8,4,8,33,8]{4,2,3,1,0:T(8,128)} fusion(pred[8,33]{0,1:T(8,128)(4,1)S(1)} %copy-done.15, bf16[16,8,3,3,3]{0,1,4,3,2:T(8,128)(2,1)S(1)} %copy-done, bf16[16,10,6,1,7,2]{0,4,5,2,1,3:T(8,128)(2,1)S(1)} %slice.97, bf16[16,10,6,1,8,33]{0,4,5,2,1,3:T(8,128)(2,1)} %copy.368), kind=kOutput, calls=%fused_computation.41 | convolution fusion | flops 60072960 | bytes 811272 | tf_op jit(solution)/shard_map/conv_general_dilated | solution.py:73
  355.0 3.5 copy.369
  361.5 6.9 reshape.443
  368.4 37.0 %all-to-all-start.8 = ((f32[32,1,2048]{2,1,0:T(1,128)}), f32[32,1,2048]{2,1,0:T(1,128)S(1)}, u32[]{:S(2)}, u32[]{:S(2)}) async-start(f32[32,1,2048]{2,1,0:T(1,128)} %reshape.443), calls=%async_computation.8 | async-start | bytes 524288 | tf_op jit(solution)/shard_map/all_to_all | solution.py:47
  405.4 3.9 fusion.35
  409.3 3.7 copy.391
  414.7 4.5 copy.388
  420.6 3.9 collective-permute-start.14
  427.8 6.4 reshape.444
  434.2 3.7 copy.436
  437.8 5.4 convolution_bitcast_fusion.5
  446.6 12.3 %all-to-all-start.9 = ((f32[32,1,2048]{2,1,0:T(1,128)}), f32[32,1,2048]{2,1,0:T(1,128)S(1)}, u32[]{:S(2)}, u32[]{:S(2)}) async-start(f32[32,1,2048]{2,1,0:T(1,128)} %reshape.445), calls=%async_computation.9 | async-start | bytes 524288 | tf_op jit(solution)/shard_map/all_to_all | solution.py:51
  458.9 22.9 %fusion.52 = f32[16,8,3,3,3]{0,1,4,3,2:T(8,128)} fusion(bf16[8,4,8,33,16]{4,2,3,1,0:T(8,128)(2,1)S(1)} %copy-done.5, pred[8,33]{0,1:T(8,128)(4,1)S(1)} %copy-done.15, bf16[8,10,6,8,33,1]{3,0,5,4,2,1:T(8,128)(2,1)} %fusion.33, bf16[8,10,6,8,33,1]{3,0,5,4,2,1:T(8,128)(2,1)} %copy.388, bf16[8,10,6,8,33,1]{3,0,5,4,2,1:T(8,128)(2,1)} %fusion.35), kind=kOutput, calls=%fused_computation.59 | convolution fusion | flops 59288064 | bytes 1044744 | tf_op jit(solution)/shard_map/transpose | solution.py:92
  482.8 12.0 %copy.395 = bf16[1,16,10,6,256]{1,0,4,3,2:T(2,128)(2,1)} copy(bf16[1,16,10,6,256]{4,1,3,2,0:T(8,128)(2,1)S(1)} %pad_maximum_fusion.7) | data formatting | bytes 983040 | tf_op jit(solution)/shard_map/concatenate | solution.py:21
  498.6 5.5 all-to-all-start.10
  504.1 90.1 %fusion.123 = f32[8,16,3,3,3]{1,0,4,3,2:T(8,128)S(1)} fusion(bf16[1,16,10,6,256]{1,0,4,3,2:T(2,128)(2,1)} %copy.395, bf16[1,8,8,4,256]{1,0,4,3,2:T(2,128)(2,1)} %copy.396), kind=kOutput, calls=%fused_computation.182 | convolution fusion | flops 56475648 | bytes 636416 | tf_op jit(solution)/shard_map/transpose | solution.py:92
  594.2 82.3 %all-reduce = (f32[16,8,3,3,3]{0,1,4,3,2:T(8,128)S(1)}, f32[8,16,3,3,3]{1,0,4,3,2:T(8,128)S(1)}) all-reduce(f32[16,8,3,3,3]{0,1,4,3,2:T(8,128)S(1)} %copy-done.11, f32[8,16,3,3,3]{1,0,4,3,2:T(8,128)S(1)} %fusion.123), channel_id=1, replica_groups=mesh['gy'=32,'gz'=8] {'gy','gz'}, use_global_device_ids=true, to_apply=%region_0.1 | all-reduce | flops 6912 | bytes 55296 | tf_op jit(solution)/shard_map/psum | solution.py:123
  677.9 5.0 copy.428
  682.8 9.3 %reshape.447 = bf16[8,2,4096]{2,1,0:T(2,128)(2,1)} reshape(bf16[8192,1,2,4]{3,2,1,0:T(2,128)(2,1)} %bitcast.304) | data formatting | bytes 262144
  692.1 4.0 all-to-all-start.11
  696.8 5.2 all-to-all-done.11
  701.9 10.0 %reshape.448 = bf16[8192,1,2,4]{3,2,1,0:T(2,128)(2,1)} reshape(bf16[8,2,4096]{2,1,0:T(2,128)(2,1)S(1)} %all-to-all-done.11) | data formatting | bytes 262144
  712.0 9.6 %copy.381 = f32[2,4,8,4,256]{4,3,2,1,0:T(4,128)S(1)} copy(bf16[2,4,8,4,256]{1,0,4,3,2:T(2,128)(2,1)} %bitcast.305) | data formatting | bytes 393216 | tf_op jit(solution)/shard_map/convert_element_type | solution.py:64
  (172 shorter events, 93.0 us)
Async XLA Ops:
  0.6 268.4 %copy-start = (bf16[16,8,3,3,3]{0,1,4,3,2:T(8,128)(2,1)S(1)}, bf16[16,8,3,3,3]{0,1,4,3,2:T(8,128)(2,1)}, u32[]{:S(2)}) copy-start(bf16[16,8,3,3,3]{0,1,4,3,2:T(8,128)(2,1)} %param.8) | copy-start | bytes 20740
  0.6 25.9 %copy-start.6 = (f32[2,4,8,4,256]{4,3,2,1,0:T(4,128)S(1)}, f32[2,4,8,4,256]{4,3,2,1,0:T(4,128)}, u32[]{:S(2)}) copy-start(f32[2,4,8,4,256]{4,3,2,1,0:T(4,128)} %param.7) | copy-start | bytes 786436
  12.1 26.5 %all-to-all-start.4 = ((f32[32,1,2048]{2,1,0:T(1,128)}), f32[32,1,2048]{2,1,0:T(1,128)S(1)}, u32[]{:S(2)}, u32[]{:S(2)}) async-start(f32[32,1,2048]{2,1,0:T(1,128)} %reshape.431), calls=%async_computation.4 | async-start | bytes 524288 | tf_op jit(solution)/shard_map/all_to_all | solution.py:47
  38.5 29.9 %all-to-all-start = ((f32[32,1,2048]{2,1,0:T(1,128)}), f32[32,1,2048]{2,1,0:T(1,128)S(1)}, u32[]{:S(2)}, u32[]{:S(2)}) async-start(f32[32,1,2048]{2,1,0:T(1,128)} %reshape.437), calls=%async_computation | async-start | bytes 524288 | tf_op jit(solution)/shard_map/all_to_all | solution.py:47
  68.4 27.1 %all-to-all-start.5 = ((f32[32,1,2048]{2,1,0:T(1,128)}), f32[32,1,2048]{2,1,0:T(1,128)S(1)}, u32[]{:S(2)}, u32[]{:S(2)}) async-start(f32[32,1,2048]{2,1,0:T(1,128)} %reshape.433), calls=%async_computation.5 | async-start | bytes 524288 | tf_op jit(solution)/shard_map/all_to_all | solution.py:51
  95.5 23.8 %all-to-all-start.1 = ((f32[32,1,2048]{2,1,0:T(1,128)}), f32[32,1,2048]{2,1,0:T(1,128)S(1)}, u32[]{:S(2)}, u32[]{:S(2)}) async-start(f32[32,1,2048]{2,1,0:T(1,128)} %reshape.439), calls=%async_computation.1 | async-start | bytes 524288 | tf_op jit(solution)/shard_map/all_to_all | solution.py:51
  119.2 16.2 %all-to-all-start.6 = ((f32[2,4,8,1024]{3,1,0,2:T(4,128)}), f32[2,4,8,1024]{3,1,0,2:T(4,128)S(1)}, u32[]{:S(2)}, u32[]{:S(2)}) async-start(f32[2,4,8,1024]{3,1,0,2:T(4,128)} %reshape.424), calls=%async_computation.6 | async-start | bytes 524288 | tf_op jit(solution)/shard_map/all_to_all | solution.py:50
  135.4 20.6 %all-to-all-start.2 = ((f32[2,4,8,1024]{3,1,0,2:T(4,128)}), f32[2,4,8,1024]{3,1,0,2:T(4,128)S(1)}, u32[]{:S(2)}, u32[]{:S(2)}) async-start(f32[2,4,8,1024]{3,1,0,2:T(4,128)} %reshape.422), calls=%async_computation.2 | async-start | bytes 524288 | tf_op jit(solution)/shard_map/all_to_all | solution.py:50
  156.0 20.8 %all-to-all-start.7 = ((bf16[8,2,4096]{2,1,0:T(2,128)(2,1)}), bf16[8,2,4096]{2,1,0:T(2,128)(2,1)S(1)}, u32[]{:S(2)}, u32[]{:S(2)}) async-start(bf16[8,2,4096]{2,1,0:T(2,128)(2,1)} %reshape.435), calls=%async_computation.7 | async-start | bytes 262144 | tf_op jit(solution)/shard_map/all_to_all | solution.py:62
  162.4 19.4 %copy-start.13 = (s32[8,4]{0,1:T(4,128)S(1)}, s32[8,4]{0,1:T(4,128)}, u32[]{:S(2)}) copy-start(s32[8,4]{0,1:T(4,128)} %param.11) | copy-start | bytes 388
  176.7 26.5 %all-to-all-start.3 = ((bf16[8,2,4096]{2,1,0:T(2,128)(2,1)}), bf16[8,2,4096]{2,1,0:T(2,128)(2,1)S(1)}, u32[]{:S(2)}, u32[]{:S(2)}) async-start(bf16[8,2,4096]{2,1,0:T(2,128)(2,1)} %reshape.441), calls=%async_computation.3 | async-start | bytes 262144 | tf_op jit(solution)/shard_map/all_to_all | solution.py:62
  201.4 34.8 %collective-permute-start.4 = (bf16[1,8,1,4,256]{4,3,2,1,0:T(4,128)(2,1)S(1)}, bf16[1,8,1,4,256]{4,3,2,1,0:T(4,128)(2,1)S(1)}, u32[]{:S(2)}, u32[]{:S(2)}) collective-permute-start(bf16[1,8,1,4,256]{4,3,2,1,0:T(4,128)(2,1)S(1)} %get-tuple-element.30), channel_id=1, source_target_pairs={{0,8},{8,16},{16,24},{24,32},{32,40},{40,48},{48,56},{56,64},{64,7... | collective-permute-start | bytes 49160 | tf_op jit(solution)/shard_map/ppermute | solution.py:19
  229.6 6.7 collective-permute-start.5
  230.9 11.9 %collective-permute-start = (bf16[1,8,1,4,256]{4,3,2,1,0:T(4,128)(2,1)S(1)}, bf16[1,8,1,4,256]{4,3,2,1,0:T(4,128)(2,1)S(1)}, u32[]{:S(2)}, u32[]{:S(2)}) collective-permute-start(bf16[1,8,1,4,256]{4,3,2,1,0:T(4,128)(2,1)S(1)} %get-tuple-element.28), channel_id=1, source_target_pairs={{0,8},{8,16},{16,24},{24,32},{32,40},{40,48},{48,56},{56,64},{64,7... | collective-permute-start | bytes 49160 | tf_op jit(solution)/shard_map/ppermute | solution.py:19
  234.9 8.0 %collective-permute-start.1 = (bf16[1,8,1,4,256]{4,3,2,1,0:T(4,128)(2,1)S(1)}, bf16[1,8,1,4,256]{4,3,2,1,0:T(4,128)(2,1)S(1)}, u32[]{:S(2)}, u32[]{:S(2)}) collective-permute-start(bf16[1,8,1,4,256]{4,3,2,1,0:T(4,128)(2,1)S(1)} %get-tuple-element.27), channel_id=1, source_target_pairs={{8,0},{16,8},{24,16},{32,24},{40,32},{48,40},{56,48},{64,56},{72,6... | collective-permute-start | bytes 49160 | tf_op jit(solution)/shard_map/ppermute | solution.py:20
  236.5 12.8 %collective-permute-start.6 = (bf16[1,8,10,1,256]{4,3,2,1,0:T(2,128)(2,1)S(1)}, bf16[1,8,10,1,256]{4,3,2,1,0:T(2,128)(2,1)S(1)}, u32[]{:S(2)}, u32[]{:S(2)}) collective-permute-start(bf16[1,8,10,1,256]{4,3,2,1,0:T(2,128)(2,1)S(1)} %get-tuple-element.25), channel_id=1, source_target_pairs={{0,1},{1,2},{2,3},{3,4},{4,5},{5,6},{6,7},{8,9},{9,10},{10,11},{11... | collective-permute-start | bytes 122888 | tf_op jit(solution)/shard_map/ppermute | solution.py:19
  240.9 8.4 %collective-permute-start.7 = (bf16[1,8,10,1,256]{4,3,2,1,0:T(2,128)(2,1)S(1)}, bf16[1,8,10,1,256]{4,3,2,1,0:T(2,128)(2,1)S(1)}, u32[]{:S(2)}, u32[]{:S(2)}) collective-permute-start(bf16[1,8,10,1,256]{4,3,2,1,0:T(2,128)(2,1)S(1)} %get-tuple-element.26), channel_id=1, source_target_pairs={{1,0},{2,1},{3,2},{4,3},{5,4},{6,5},{7,6},{9,8},{10,9},{11,10},{12... | collective-permute-start | bytes 122888 | tf_op jit(solution)/shard_map/ppermute | solution.py:20
  243.7 17.3 %collective-permute-start.2 = (bf16[1,8,10,1,256]{4,3,2,1,0:T(2,128)(2,1)}, bf16[1,8,10,1,256]{4,3,2,1,0:T(2,128)(2,1)}, u32[]{:S(2)}, u32[]{:S(2)}) collective-permute-start(bf16[1,8,10,1,256]{4,3,2,1,0:T(2,128)(2,1)} %get-tuple-element.23), channel_id=1, source_target_pairs={{0,1},{1,2},{2,3},{3,4},{4,5},{5,6},{6,7},{8,9},{9,10},{10,11},{11... | collective-permute-start | bytes 122888 | tf_op jit(solution)/shard_map/ppermute | solution.py:19
  247.3 13.7 %collective-permute-start.3 = (bf16[1,8,10,1,256]{4,3,2,1,0:T(2,128)(2,1)}, bf16[1,8,10,1,256]{4,3,2,1,0:T(2,128)(2,1)}, u32[]{:S(2)}, u32[]{:S(2)}) collective-permute-start(bf16[1,8,10,1,256]{4,3,2,1,0:T(2,128)(2,1)} %get-tuple-element.24), channel_id=1, source_target_pairs={{1,0},{2,1},{3,2},{4,3},{5,4},{6,5},{7,6},{9,8},{10,9},{11,10},{12... | collective-permute-start | bytes 122888 | tf_op jit(solution)/shard_map/ppermute | solution.py:20
  261.0 8.0 %copy-start.15 = (pred[8,33]{0,1:T(8,128)(4,1)S(1)}, pred[8,33]{0,1:T(8,128)(4,1)}, u32[]{:S(2)}) copy-start(pred[8,33]{0,1:T(8,128)(4,1)} %constant.88) | copy-start | bytes 796
  262.2 6.8 copy-start.8
  269.0 9.1 %copy-start.2 = (bf16[8,10,6,1,8,33]{0,4,5,2,1,3:T(8,128)(2,1)S(1)}, bf16[8,10,6,1,8,33]{0,4,5,2,1,3:T(8,128)(2,1)}, u32[]{:S(2)}) copy-start(bf16[8,10,6,1,8,33]{0,4,5,2,1,3:T(8,128)(2,1)} %copy.347) | copy-start | bytes 760324
  269.0 9.1 %copy-start.14 = (bf16[8,16,3,3,3]{1,0,4,3,2:T(8,128)(2,1)S(1)}, bf16[8,16,3,3,3]{1,0,4,3,2:T(8,128)(2,1)}, u32[]{:S(2)}) copy-start(bf16[8,16,3,3,3]{1,0,4,3,2:T(8,128)(2,1)} %param.9) | copy-start | bytes 20740
  296.9 122.3 %collective-permute-start.12 = (bf16[1,16,1,4,256]{4,1,3,0,2:T(8,128)(2,1)}, bf16[1,16,1,4,256]{4,1,3,0,2:T(8,128)(2,1)}, u32[]{:S(2)}, u32[]{:S(2)}) collective-permute-start(bf16[1,16,1,4,256]{4,1,3,0,2:T(8,128)(2,1)} %slice_bitcast_fusion.4), channel_id=1, source_target_pairs={{0,8},{8,16},{16,24},{24,32},{32,40},{40,48},{48,56},{56,64},{64,7... | collective-permute-start | bytes 98312 | tf_op jit(solution)/shard_map/ppermute | solution.py:19
  303.2 116.0 %collective-permute-start.13 = (bf16[1,16,1,4,256]{4,1,3,0,2:T(8,128)(2,1)}, bf16[1,16,1,4,256]{4,1,3,0,2:T(8,128)(2,1)}, u32[]{:S(2)}, u32[]{:S(2)}) collective-permute-start(bf16[1,16,1,4,256]{4,1,3,0,2:T(8,128)(2,1)} %slice_bitcast_fusion.3), channel_id=1, source_target_pairs={{8,0},{16,8},{24,16},{32,24},{40,32},{48,40},{56,48},{64,56},{72,6... | collective-permute-start | bytes 98312 | tf_op jit(solution)/shard_map/ppermute | solution.py:20
  305.2 12.1 %copy-start.4 = (bf16[8,10,6,1,7,1]{5,4,2,1,0,3:T(8,128)(2,1)S(1)}, bf16[8,10,6,1,7,1]{5,4,2,1,0,3:T(8,128)(2,1)}, u32[]{:S(2)}) copy-start(bf16[8,10,6,1,7,1]{5,4,2,1,0,3:T(8,128)(2,1)} %get-tuple-element.12) | copy-start | bytes 20164
  306.7 13.5 %collective-permute-start.8 = (bf16[1,16,1,4,256]{4,1,3,0,2:T(8,128)(2,1)S(1)}, bf16[1,16,1,4,256]{4,1,3,0,2:T(8,128)(2,1)S(1)}, u32[]{:S(2)}, u32[]{:S(2)}) collective-permute-start(bf16[1,16,1,4,256]{4,1,3,0,2:T(8,128)(2,1)S(1)} %slice_bitcast_fusion.6), channel_id=1, source_target_pairs={{0,8},{8,16},{16,24},{24,32},{32,40},{40,48},{48,56},{56,64},{64,7... | collective-permute-start | bytes 98312 | tf_op jit(solution)/shard_map/ppermute | solution.py:19
  311.2 9.1 %collective-permute-start.9 = (bf16[1,16,1,4,256]{4,1,3,2,0:T(8,128)(2,1)S(1)}, bf16[1,16,1,4,256]{4,1,3,2,0:T(8,128)(2,1)S(1)}, u32[]{:S(2)}, u32[]{:S(2)}) collective-permute-start(bf16[1,16,1,4,256]{4,1,3,2,0:T(8,128)(2,1)S(1)} %slice_bitcast_fusion.5), channel_id=1, source_target_pairs={{8,0},{16,8},{24,16},{32,24},{40,32},{48,40},{56,48},{64,56},{72,6... | collective-permute-start | bytes 98312 | tf_op jit(solution)/shard_map/ppermute | solution.py:20
  320.3 16.8 %collective-permute-start.10 = (bf16[1,16,10,1,256]{4,1,3,2,0:T(8,128)(2,1)S(1)}, bf16[1,16,10,1,256]{4,1,3,2,0:T(8,128)(2,1)S(1)}, u32[]{:S(2)}, u32[]{:S(2)}) collective-permute-start(bf16[1,16,10,1,256]{4,1,3,2,0:T(8,128)(2,1)S(1)} %get-tuple-element.17), channel_id=1, source_target_pairs={{0,1},{1,2},{2,3},{3,4},{4,5},{5,6},{6,7},{8,9},{9,10},{10,11},{11... | collective-permute-start | bytes 245768 | tf_op jit(solution)/shard_map/ppermute | solution.py:19
  324.8 12.3 %collective-permute-start.11 = (bf16[1,16,10,1,256]{4,1,3,2,0:T(8,128)(2,1)S(1)}, bf16[1,16,10,1,256]{4,1,3,2,0:T(8,128)(2,1)}, u32[]{:S(2)}, u32[]{:S(2)}) collective-permute-start(bf16[1,16,10,1,256]{4,1,3,2,0:T(8,128)(2,1)S(1)} %get-tuple-element.18), channel_id=1, source_target_pairs={{1,0},{2,1},{3,2},{4,3},{5,4},{6,5},{7,6},{9,8},{10,9},{11,10},{12... | collective-permute-start | bytes 245768 | tf_op jit(solution)/shard_map/ppermute | solution.py:20
  330.7 3.5 copy-start.3
  368.4 58.1 %all-to-all-start.8 = ((f32[32,1,2048]{2,1,0:T(1,128)}), f32[32,1,2048]{2,1,0:T(1,128)S(1)}, u32[]{:S(2)}, u32[]{:S(2)}) async-start(f32[32,1,2048]{2,1,0:T(1,128)} %reshape.443), calls=%async_computation.8 | async-start | bytes 524288 | tf_op jit(solution)/shard_map/all_to_all | solution.py:47
  420.6 61.2 %collective-permute-start.14 = (bf16[1,16,10,1,256]{4,1,3,2,0:T(8,128)(2,1)}, bf16[1,16,10,1,256]{4,1,3,2,0:T(8,128)(2,1)}, u32[]{:S(2)}, u32[]{:S(2)}) collective-permute-start(bf16[1,16,10,1,256]{4,1,3,2,0:T(8,128)(2,1)} %get-tuple-element.13), channel_id=1, source_target_pairs={{0,1},{1,2},{2,3},{3,4},{4,5},{5,6},{6,7},{8,9},{9,10},{10,11},{11... | collective-permute-start | bytes 245768 | tf_op jit(solution)/shard_map/ppermute | solution.py:19
  424.5 57.3 %collective-permute-start.15 = (bf16[1,16,10,1,256]{4,1,3,2,0:T(8,128)(2,1)}, bf16[1,16,10,1,256]{4,1,3,2,0:T(8,128)(2,1)}, u32[]{:S(2)}, u32[]{:S(2)}) collective-permute-start(bf16[1,16,10,1,256]{4,1,3,2,0:T(8,128)(2,1)} %get-tuple-element.14), channel_id=1, source_target_pairs={{1,0},{2,1},{3,2},{4,3},{5,4},{6,5},{7,6},{9,8},{10,9},{11,10},{12... | collective-permute-start | bytes 245768 | tf_op jit(solution)/shard_map/ppermute | solution.py:20
  434.2 24.7 %copy-start.5 = (bf16[8,4,8,33,16]{4,2,3,1,0:T(8,128)(2,1)S(1)}, bf16[8,4,8,33,16]{4,2,3,1,0:T(8,128)(2,1)}, u32[]{:S(2)}) copy-start(bf16[8,4,8,33,16]{4,2,3,1,0:T(8,128)(2,1)} %multiply_convert_fusion) | copy-start | bytes 811012
  446.6 48.2 %all-to-all-start.9 = ((f32[32,1,2048]{2,1,0:T(1,128)}), f32[32,1,2048]{2,1,0:T(1,128)S(1)}, u32[]{:S(2)}, u32[]{:S(2)}) async-start(f32[32,1,2048]{2,1,0:T(1,128)} %reshape.445), calls=%async_computation.9 | async-start | bytes 524288 | tf_op jit(solution)/shard_map/all_to_all | solution.py:51
  498.6 178.5 %all-to-all-start.10 = ((f32[2,4,8,1024]{3,1,0,2:T(4,128)}), f32[2,4,8,1024]{3,1,0,2:T(4,128)S(1)}, u32[]{:S(2)}, u32[]{:S(2)}) async-start(f32[2,4,8,1024]{3,1,0,2:T(4,128)} %reshape.426), calls=%async_computation.10 | async-start | bytes 524288 | tf_op jit(solution)/shard_map/all_to_all | solution.py:50
  504.1 90.1 %copy-start.11 = (f32[16,8,3,3,3]{0,1,4,3,2:T(8,128)S(1)}, f32[16,8,3,3,3]{0,1,4,3,2:T(8,128)}, u32[]{:S(2)}) copy-start(f32[16,8,3,3,3]{0,1,4,3,2:T(8,128)} %fusion.52) | copy-start | bytes 41476
  504.1 173.3 %copy-start.9 = (f32[1,2,32,32]{3,2,1,0:T(8,128)S(1)}, f32[1,2,32,32]{3,2,1,0:T(8,128)}, u32[]{:S(2)}) copy-start(f32[1,2,32,32]{3,2,1,0:T(8,128)} %get-tuple-element.31) | copy-start | bytes 24580
  504.1 173.3 %copy-start.10 = (f32[1,2,32,32]{3,2,1,0:T(8,128)S(1)}, f32[1,2,32,32]{3,2,1,0:T(8,128)}, u32[]{:S(2)}) copy-start(f32[1,2,32,32]{3,2,1,0:T(8,128)} %get-tuple-element.32) | copy-start | bytes 24580
  692.1 9.8 %all-to-all-start.11 = ((bf16[8,2,4096]{2,1,0:T(2,128)(2,1)}), bf16[8,2,4096]{2,1,0:T(2,128)(2,1)S(1)}, u32[]{:S(2)}, u32[]{:S(2)}) async-start(bf16[8,2,4096]{2,1,0:T(2,128)(2,1)} %reshape.447), calls=%async_computation.11 | async-start | bytes 262144 | tf_op jit(solution)/shard_map/all_to_all | solution.py:62
  696.1 26.4 %copy-start.1 = (bf16[16,8,3,3,3]{0,1,4,3,2:T(8,128)(2,1)S(1)}, bf16[16,8,3,3,3]{0,1,4,3,2:T(8,128)(2,1)}, u32[]{:S(2)}) copy-start(bf16[16,8,3,3,3]{0,1,4,3,2:T(8,128)(2,1)} %param.8) | copy-start | bytes 20740
  696.8 24.9 %copy-start.7 = (f32[2,4,8,4,256]{4,3,2,1,0:T(4,128)S(1)}, f32[2,4,8,4,256]{4,3,2,1,0:T(4,128)}, u32[]{:S(2)}) copy-start(f32[2,4,8,4,256]{4,3,2,1,0:T(4,128)} %param.7) | copy-start | bytes 786436
  696.8 24.9 %copy-start.12 = (f32[8,4]{1,0:T(8,128)S(1)}, f32[8,4]{1,0:T(8,128)}, u32[]{:S(2)}) copy-start(f32[8,4]{1,0:T(8,128)} %copy.333) | copy-start | bytes 388
where the time goes:
time: 732 us; the launch traced here: 723 us
  local copies, waits for them, and re-layouts  264 us (36%)
  starting transfers between devices  175 us (24%)
  matrix products  151 us (21%)
  blocking collectives  82.3 us (11%)
  other arithmetic  28 us (4%)
  waiting for transfers between devices  19.7 us (3%)
    unnamed x60, local copies, waits for them, and re-layouts  126 us
    transpose x2, matrix products, kernel_gradient(): return summed.transpose(1, 0, 2, 3, 4)  113 us
    psum x1, blocking collectives, local(): summed_in, summed_out = lax.psum((local_in, local_out), ('gy', 'gz'))  82.3 us
    all_to_all x3, starting transfers between devices, spectral(): lax.all_to_all(flattened, 'gy', split_axis=3, concat_axis=2, tiled=True)  62.5 us
    all_to_all x3, starting transfers between devices, spectral(): lax.all_to_all(transformed_y, 'gy', split_axis=2, concat_axis=3, tiled=True)  36.1 us
    ppermute x8, starting transfers between devices, extended(): before = lax.ppermute(last, axis, up)  31.5 us
    conv_general_dilated x3, matrix products, convolve(): lax.conv_general_dilated(padded, kernel, (1, 1, 1), ((0, 0), (0, 0), (1,...  27.8 us
    conv_general_dilated x12, local copies, waits for them, and re-layouts, convolve(): lax.conv_general_dilated(padded, kernel, (1, 1, 1), ((0, 0), (0, 0), (1,...  25.1 us
  transfers between devices with their start and end apart: 28, of which 4 were waited for; matrix products, arithmetic and copies ran while one was open for 49% of the time, Pallas kernels for 0%

commit v1 on v0

--- a/solution.py
+++ b/solution.py
@@ -120,7 +120,7 @@
     hidden_padded = with_rims(back_hidden)
     back_image = convolve(hidden_padded, flipped(weight_in))
     spectrum = spectral(back_image.reshape(2, coil_count, cells_y, cells_z, readout), -1.0)
-    summed_in, summed_out = lax.psum((local_in, local_out), ("gy", "gz"))
+    summed_in, summed_out = lax.psum(lax.psum((local_in, local_out), "gy"), "gz")
     scale = 1.0 / math.sqrt(voxels)
     mask_field = sampling_mask.astype(jnp.float32)[None, None, :, :, None]
     grad_kspace = cotangent - consistency_weight[0] * mask_field * cotangent + spectrum

time: 732 us -> 903 us (1.23)
  blocking collectives: 82.3 us -> 251 us
    psum x1 -> x2, blocking collectives: 82.3 us -> 251 us  [the longest x1 199 us: local(): lax.psum((local_in, local_out), 'gy')]
  transfers between devices with their start and end apart: 28 -> 28, of which waited for: 4 -> 4; matrix products, arithmetic and copies ran while one was open for 49% -> 40% of each run, Pallas kernels for 0% -> 0%
where the time goes in v1:
time: 903 us; the launch traced here: 895 us
  local copies, waits for them, and re-layouts  264 us (29%)
  blocking collectives  251 us (28%)
  starting transfers between devices  178 us (20%)
  matrix products  152 us (17%)
  other arithmetic  27.7 us (3%)
  waiting for transfers between devices  19.8 us (2%)
    psum x1, blocking collectives, local(): lax.psum((local_in, local_out), 'gy')  199 us
    unnamed x60, local copies, waits for them, and re-layouts  126 us
    transpose x2, matrix products, kernel_gradient(): return summed.transpose(1, 0, 2, 3, 4)  113 us
    all_to_all x3, starting transfers between devices, spectral(): lax.all_to_all(flattened, 'gy', split_axis=3, concat_axis=2, tiled=True)  62.5 us
    psum x1, blocking collectives, local(): lax.psum(lax.psum((local_in, local_out), 'gy'), 'gz')  52.4 us
    all_to_all x3, starting transfers between devices, spectral(): lax.all_to_all(transformed_y, 'gy', split_axis=2, concat_axis=3, tiled=True)  36.1 us
    ppermute x8, starting transfers between devices, extended(): before = lax.ppermute(last, axis, up)  31.5 us
    conv_general_dilated x3, matrix products, convolve(): lax.conv_general_dilated(padded, kernel, (1, 1, 1), ((0, 0), (0, 0), (1,...  27.8 us
  transfers between devices with their start and end apart: 28, of which 4 were waited for; matrix products, arithmetic and copies ran while one was open for 40% of the time, Pallas kernels for 0%

profile of v1, /device:TPU:1, one launch (start us, length us, event | category | flops | bytes accessed | tf_op | source)
XLA Modules:
  0.0 894.5 jit_solution(17645300207764178170)
XLA Ops:
  0.7 4.5 copy.348
  5.1 6.9 reshape.431
  12.0 14.5 %all-to-all-start.4 = ((f32[32,1,2048]{2,1,0:T(1,128)}), f32[32,1,2048]{2,1,0:T(1,128)S(1)}, u32[]{:S(2)}, u32[]{:S(2)}) async-start(f32[32,1,2048]{2,1,0:T(1,128)} %reshape.431), calls=%async_computation.4 | async-start | bytes 524288 | tf_op jit(solution)/shard_map/all_to_all | solution.py:47
  29.7 6.9 reshape.437
  38.5 11.0 %all-to-all-start = ((f32[32,1,2048]{2,1,0:T(1,128)}), f32[32,1,2048]{2,1,0:T(1,128)S(1)}, u32[]{:S(2)}, u32[]{:S(2)}) async-start(f32[32,1,2048]{2,1,0:T(1,128)} %reshape.437), calls=%async_computation | async-start | bytes 524288 | tf_op jit(solution)/shard_map/all_to_all | solution.py:47
  54.5 6.3 reshape.432
  60.9 3.5 copy.417
  68.3 12.0 %all-to-all-start.5 = ((f32[32,1,2048]{2,1,0:T(1,128)}), f32[32,1,2048]{2,1,0:T(1,128)S(1)}, u32[]{:S(2)}, u32[]{:S(2)}) async-start(f32[32,1,2048]{2,1,0:T(1,128)} %reshape.433), calls=%async_computation.5 | async-start | bytes 524288 | tf_op jit(solution)/shard_map/all_to_all | solution.py:51
  81.5 6.3 reshape.438
  87.9 3.5 copy.411
  95.3 11.8 %all-to-all-start.1 = ((f32[32,1,2048]{2,1,0:T(1,128)}), f32[32,1,2048]{2,1,0:T(1,128)S(1)}, u32[]{:S(2)}, u32[]{:S(2)}) async-start(f32[32,1,2048]{2,1,0:T(1,128)} %reshape.439), calls=%async_computation.1 | async-start | bytes 524288 | tf_op jit(solution)/shard_map/all_to_all | solution.py:51
  110.5 8.6 all-to-all-done.1
  119.1 7.4 all-to-all-start.6
  130.1 5.2 all-to-all-done.6
  135.2 4.8 all-to-all-start.2
  141.5 4.9 copy.421
  146.4 9.3 %reshape.435 = bf16[8,2,4096]{2,1,0:T(2,128)(2,1)} reshape(bf16[8192,1,2,4]{3,2,1,0:T(2,128)(2,1)} %bitcast.299) | data formatting | bytes 262144
  155.8 5.1 all-to-all-start.7
  162.2 4.9 copy.415
  167.1 9.3 %reshape.441 = bf16[8,2,4096]{2,1,0:T(2,128)(2,1)} reshape(bf16[8192,1,2,4]{3,2,1,0:T(2,128)(2,1)} %bitcast.300) | data formatting | bytes 262144
  176.5 5.1 all-to-all-start.3
  182.3 10.0 %reshape.436 = bf16[8192,1,2,4]{3,2,1,0:T(2,128)(2,1)} reshape(bf16[8,2,4096]{2,1,0:T(2,128)(2,1)S(1)} %all-to-all-done.7) | data formatting | bytes 262144
  192.3 8.6 copy.358
  203.0 10.0 %reshape.442 = bf16[8192,1,2,4]{3,2,1,0:T(2,128)(2,1)} reshape(bf16[8,2,4096]{2,1,0:T(2,128)(2,1)S(1)} %all-to-all-done.3) | data formatting | bytes 262144
  213.0 8.6 copy.344
  221.9 7.4 copy.396
  230.6 4.0 collective-permute-start
  236.1 4.4 collective-permute-start.6
  243.3 3.6 collective-permute-start.2
  254.2 4.8 copy.361
  262.9 4.6 copy.347
  268.7 9.1 %multiply_convert_fusion.1 = (bf16[8,4,8,33,16]{4,2,3,1,0:T(8,128)(2,1)}, f32[8,4,8,33,16]{4,2,3,1,0:T(8,128)S(1)}) fusion(pred[8,33]{0,1:T(8,128)(4,1)S(1)} %copy-done.15, bf16[16,8,3,3,3]{0,1,4,3,2:T(8,128)(2,1)S(1)} %copy-done, bf16[8,10,6,1,7,2]{0,4,5,2,1,3:T(8,128)(2,1)S(1)} %copy-done.8, bf16[8,10,6,1,8,33]{0,4,5,2,1,3:T(8,128)(2,1)} %copy.361), kind=kOutput, calls=%fused_computation.16 | convolution fusion | flops 60009984 | bytes 1085064 | tf_op jit(solution)/shard_map/conv_general_dilated | solution.py:73
  277.8 9.5 %multiply_convert_fusion = bf16[8,4,8,33,16]{4,2,3,1,0:T(8,128)(2,1)} fusion(f32[8,4,8,33,16]{4,2,3,1,0:T(8,128)S(1)} %get-tuple-element.38, bf16[8,16,3,3,3]{1,0,4,3,2:T(8,128)(2,1)S(1)} %copy-done.14, bf16[8,10,6,1,7,2]{0,4,5,2,1,3:T(8,128)(2,1)S(1)} %slice.86, bf16[8,10,6,1,8,33]{0,4,5,2,1,3:T(8,128)(2,1)S(1)} %copy-done.2, pred[8,33]{0,1:T(8,128)(4,1)S(1)} %copy-done.15), kind=kOutput, calls=%fused_computation.15 | convolution fusion | flops 60685824 | bytes 1085064 | tf_op jit(solution)/shard_map/conv_general_dilated | solution.py:73
  287.3 3.7 copy.363
  296.5 5.3 collective-permute-start.12
  306.4 4.0 collective-permute-start.8
  312.1 4.8 copy.442
  319.9 4.5 collective-permute-start.10
  326.3 4.0 fusion.33
  330.3 3.5 copy.441
  339.8 4.8 copy.368
  345.6 9.1 %broadcast_select_fusion = f32[8,4,8,33,8]{4,2,3,1,0:T(8,128)} fusion(pred[8,33]{0,1:T(8,128)(4,1)S(1)} %copy-done.15, bf16[16,8,3,3,3]{0,1,4,3,2:T(8,128)(2,1)S(1)} %copy-done, bf16[16,10,6,1,7,2]{0,4,5,2,1,3:T(8,128)(2,1)S(1)} %slice.97, bf16[16,10,6,1,8,33]{0,4,5,2,1,3:T(8,128)(2,1)} %copy.368), kind=kOutput, calls=%fused_computation.41 | convolution fusion | flops 60072960 | bytes 811272 | tf_op jit(solution)/shard_map/conv_general_dilated | solution.py:73
  361.2 6.9 reshape.443
  368.1 37.0 %all-to-all-start.8 = ((f32[32,1,2048]{2,1,0:T(1,128)}), f32[32,1,2048]{2,1,0:T(1,128)S(1)}, u32[]{:S(2)}, u32[]{:S(2)}) async-start(f32[32,1,2048]{2,1,0:T(1,128)} %reshape.443), calls=%async_computation.8 | async-start | bytes 524288 | tf_op jit(solution)/shard_map/all_to_all | solution.py:47
  405.1 3.9 fusion.35
  409.0 3.7 copy.391
  414.4 4.5 copy.388
  420.4 3.9 collective-permute-start.14
  427.5 6.4 reshape.444
  433.9 3.7 copy.436
  437.5 5.4 convolution_bitcast_fusion.5
  446.3 12.3 %all-to-all-start.9 = ((f32[32,1,2048]{2,1,0:T(1,128)}), f32[32,1,2048]{2,1,0:T(1,128)S(1)}, u32[]{:S(2)}, u32[]{:S(2)}) async-start(f32[32,1,2048]{2,1,0:T(1,128)} %reshape.445), calls=%async_computation.9 | async-start | bytes 524288 | tf_op jit(solution)/shard_map/all_to_all | solution.py:51
  458.6 22.9 %fusion.52 = f32[16,8,3,3,3]{0,1,4,3,2:T(8,128)} fusion(bf16[8,4,8,33,16]{4,2,3,1,0:T(8,128)(2,1)S(1)} %copy-done.5, pred[8,33]{0,1:T(8,128)(4,1)S(1)} %copy-done.15, bf16[8,10,6,8,33,1]{3,0,5,4,2,1:T(8,128)(2,1)} %fusion.33, bf16[8,10,6,8,33,1]{3,0,5,4,2,1:T(8,128)(2,1)} %copy.388, bf16[8,10,6,8,33,1]{3,0,5,4,2,1:T(8,128)(2,1)} %fusion.35), kind=kOutput, calls=%fused_computation.59 | convolution fusion | flops 59288064 | bytes 1044744 | tf_op jit(solution)/shard_map/transpose | solution.py:92
  482.5 11.9 %copy.395 = bf16[1,16,10,6,256]{1,0,4,3,2:T(2,128)(2,1)} copy(bf16[1,16,10,6,256]{4,1,3,2,0:T(8,128)(2,1)S(1)} %pad_maximum_fusion.7) | data formatting | bytes 983040 | tf_op jit(solution)/shard_map/concatenate | solution.py:21
  498.2 5.5 all-to-all-start.10
  503.7 90.1 %fusion.123 = f32[8,16,3,3,3]{1,0,4,3,2:T(8,128)S(1)} fusion(bf16[1,16,10,6,256]{1,0,4,3,2:T(2,128)(2,1)} %copy.395, bf16[1,8,8,4,256]{1,0,4,3,2:T(2,128)(2,1)} %copy.396), kind=kOutput, calls=%fused_computation.182 | convolution fusion | flops 56475648 | bytes 636416 | tf_op jit(solution)/shard_map/transpose | solution.py:92
  593.8 198.7 %all-reduce = (f32[16,8,3,3,3]{0,1,4,3,2:T(8,128)S(1)}, f32[8,16,3,3,3]{1,0,4,3,2:T(8,128)S(1)}) all-reduce(f32[16,8,3,3,3]{0,1,4,3,2:T(8,128)S(1)} %copy-done.11, f32[8,16,3,3,3]{1,0,4,3,2:T(8,128)S(1)} %fusion.123), channel_id=1, replica_groups=mesh['gy'=32,'gz'=8] {'gy'}, use_global_device_ids=true, to_apply=%region_0.1 | all-reduce | flops 6912 | bytes 55296 | tf_op jit(solution)/shard_map/psum | solution.py:123
  792.5 52.4 %all-reduce.1 = (f32[16,8,3,3,3]{0,1,4,3,2:T(8,128)S(1)}, f32[8,16,3,3,3]{1,0,4,3,2:T(8,128)S(1)}) all-reduce(f32[16,8,3,3,3]{0,1,4,3,2:T(8,128)S(1)} %get-tuple-element.3, f32[8,16,3,3,3]{1,0,4,3,2:T(8,128)S(1)} %get-tuple-element.4), channel_id=1, replica_groups=mesh['gy'=32,'gz'=8] {'gz'}, use_global_device_ids=true, to_apply=%region_1.2 | all-reduce | flops 6912 | bytes 55296 | tf_op jit(solution)/shard_map/psum | solution.py:123
  846.2 5.0 copy.428
  851.2 9.3 %reshape.447 = bf16[8,2,4096]{2,1,0:T(2,128)(2,1)} reshape(bf16[8192,1,2,4]{3,2,1,0:T(2,128)(2,1)} %bitcast.304) | data formatting | bytes 262144
  860.5 7.4 all-to-all-start.11
  868.6 5.2 all-to-all-done.11
  873.8 10.0 %reshape.448 = bf16[8192,1,2,4]{3,2,1,0:T(2,128)(2,1)} reshape(bf16[8,2,4096]{2,1,0:T(2,128)(2,1)S(1)} %all-to-all-done.11) | data formatting | bytes 262144
  883.8 9.6 %copy.381 = f32[2,4,8,4,256]{4,3,2,1,0:T(4,128)S(1)} copy(bf16[2,4,8,4,256]{1,0,4,3,2:T(2,128)(2,1)} %bitcast.305) | data formatting | bytes 393216 | tf_op jit(solution)/shard_map/convert_element_type | solution.py:64
  (173 shorter events, 96.1 us)
Async XLA Ops:
  0.6 268.0 %copy-start = (bf16[16,8,3,3,3]{0,1,4,3,2:T(8,128)(2,1)S(1)}, bf16[16,8,3,3,3]{0,1,4,3,2:T(8,128)(2,1)}, u32[]{:S(2)}) copy-start(bf16[16,8,3,3,3]{0,1,4,3,2:T(8,128)(2,1)} %param.8) | copy-start | bytes 20740
  0.6 25.9 %copy-start.6 = (f32[2,4,8,4,256]{4,3,2,1,0:T(4,128)S(1)}, f32[2,4,8,4,256]{4,3,2,1,0:T(4,128)}, u32[]{:S(2)}) copy-start(f32[2,4,8,4,256]{4,3,2,1,0:T(4,128)} %param.7) | copy-start | bytes 786436
  12.0 26.5 %all-to-all-start.4 = ((f32[32,1,2048]{2,1,0:T(1,128)}), f32[32,1,2048]{2,1,0:T(1,128)S(1)}, u32[]{:S(2)}, u32[]{:S(2)}) async-start(f32[32,1,2048]{2,1,0:T(1,128)} %reshape.431), calls=%async_computation.4 | async-start | bytes 524288 | tf_op jit(solution)/shard_map/all_to_all | solution.py:47
  38.5 29.8 %all-to-all-start = ((f32[32,1,2048]{2,1,0:T(1,128)}), f32[32,1,2048]{2,1,0:T(1,128)S(1)}, u32[]{:S(2)}, u32[]{:S(2)}) async-start(f32[32,1,2048]{2,1,0:T(1,128)} %reshape.437), calls=%async_computation | async-start | bytes 524288 | tf_op jit(solution)/shard_map/all_to_all | solution.py:47
  68.3 27.0 %all-to-all-start.5 = ((f32[32,1,2048]{2,1,0:T(1,128)}), f32[32,1,2048]{2,1,0:T(1,128)S(1)}, u32[]{:S(2)}, u32[]{:S(2)}) async-start(f32[32,1,2048]{2,1,0:T(1,128)} %reshape.433), calls=%async_computation.5 | async-start | bytes 524288 | tf_op jit(solution)/shard_map/all_to_all | solution.py:51
  95.3 23.8 %all-to-all-start.1 = ((f32[32,1,2048]{2,1,0:T(1,128)}), f32[32,1,2048]{2,1,0:T(1,128)S(1)}, u32[]{:S(2)}, u32[]{:S(2)}) async-start(f32[32,1,2048]{2,1,0:T(1,128)} %reshape.439), calls=%async_computation.1 | async-start | bytes 524288 | tf_op jit(solution)/shard_map/all_to_all | solution.py:51
  119.1 16.2 %all-to-all-start.6 = ((f32[2,4,8,1024]{3,1,0,2:T(4,128)}), f32[2,4,8,1024]{3,1,0,2:T(4,128)S(1)}, u32[]{:S(2)}, u32[]{:S(2)}) async-start(f32[2,4,8,1024]{3,1,0,2:T(4,128)} %reshape.424), calls=%async_computation.6 | async-start | bytes 524288 | tf_op jit(solution)/shard_map/all_to_all | solution.py:50
  135.2 20.5 %all-to-all-start.2 = ((f32[2,4,8,1024]{3,1,0,2:T(4,128)}), f32[2,4,8,1024]{3,1,0,2:T(4,128)S(1)}, u32[]{:S(2)}, u32[]{:S(2)}) async-start(f32[2,4,8,1024]{3,1,0,2:T(4,128)} %reshape.422), calls=%async_computation.2 | async-start | bytes 524288 | tf_op jit(solution)/shard_map/all_to_all | solution.py:50
  155.8 20.7 %all-to-all-start.7 = ((bf16[8,2,4096]{2,1,0:T(2,128)(2,1)}), bf16[8,2,4096]{2,1,0:T(2,128)(2,1)S(1)}, u32[]{:S(2)}, u32[]{:S(2)}) async-start(bf16[8,2,4096]{2,1,0:T(2,128)(2,1)} %reshape.435), calls=%async_computation.7 | async-start | bytes 262144 | tf_op jit(solution)/shard_map/all_to_all | solution.py:62
  162.2 19.4 %copy-start.13 = (s32[8,4]{0,1:T(4,128)S(1)}, s32[8,4]{0,1:T(4,128)}, u32[]{:S(2)}) copy-start(s32[8,4]{0,1:T(4,128)} %param.11) | copy-start | bytes 388
  176.5 26.5 %all-to-all-start.3 = ((bf16[8,2,4096]{2,1,0:T(2,128)(2,1)}), bf16[8,2,4096]{2,1,0:T(2,128)(2,1)S(1)}, u32[]{:S(2)}, u32[]{:S(2)}) async-start(bf16[8,2,4096]{2,1,0:T(2,128)(2,1)} %reshape.441), calls=%async_computation.3 | async-start | bytes 262144 | tf_op jit(solution)/shard_map/all_to_all | solution.py:62
  201.1 34.8 %collective-permute-start.4 = (bf16[1,8,1,4,256]{4,3,2,1,0:T(4,128)(2,1)S(1)}, bf16[1,8,1,4,256]{4,3,2,1,0:T(4,128)(2,1)S(1)}, u32[]{:S(2)}, u32[]{:S(2)}) collective-permute-start(bf16[1,8,1,4,256]{4,3,2,1,0:T(4,128)(2,1)S(1)} %get-tuple-element.32), channel_id=1, source_target_pairs={{0,8},{8,16},{16,24},{24,32},{32,40},{40,48},{48,56},{56,64},{64,7... | collective-permute-start | bytes 49160 | tf_op jit(solution)/shard_map/ppermute | solution.py:19
  229.3 6.7 collective-permute-start.5
  230.6 11.9 %collective-permute-start = (bf16[1,8,1,4,256]{4,3,2,1,0:T(4,128)(2,1)S(1)}, bf16[1,8,1,4,256]{4,3,2,1,0:T(4,128)(2,1)S(1)}, u32[]{:S(2)}, u32[]{:S(2)}) collective-permute-start(bf16[1,8,1,4,256]{4,3,2,1,0:T(4,128)(2,1)S(1)} %get-tuple-element.30), channel_id=1, source_target_pairs={{0,8},{8,16},{16,24},{24,32},{32,40},{40,48},{48,56},{56,64},{64,7... | collective-permute-start | bytes 49160 | tf_op jit(solution)/shard_map/ppermute | solution.py:19
  234.5 8.0 collective-permute-start.1
  236.1 12.8 %collective-permute-start.6 = (bf16[1,8,10,1,256]{4,3,2,1,0:T(2,128)(2,1)S(1)}, bf16[1,8,10,1,256]{4,3,2,1,0:T(2,128)(2,1)S(1)}, u32[]{:S(2)}, u32[]{:S(2)}) collective-permute-start(bf16[1,8,10,1,256]{4,3,2,1,0:T(2,128)(2,1)S(1)} %get-tuple-element.27), channel_id=1, source_target_pairs={{0,1},{1,2},{2,3},{3,4},{4,5},{5,6},{6,7},{8,9},{9,10},{10,11},{11... | collective-permute-start | bytes 122888 | tf_op jit(solution)/shard_map/ppermute | solution.py:19
  240.5 8.4 collective-permute-start.7
  243.3 17.3 %collective-permute-start.2 = (bf16[1,8,10,1,256]{4,3,2,1,0:T(2,128)(2,1)}, bf16[1,8,10,1,256]{4,3,2,1,0:T(2,128)(2,1)}, u32[]{:S(2)}, u32[]{:S(2)}) collective-permute-start(bf16[1,8,10,1,256]{4,3,2,1,0:T(2,128)(2,1)} %get-tuple-element.25), channel_id=1, source_target_pairs={{0,1},{1,2},{2,3},{3,4},{4,5},{5,6},{6,7},{8,9},{9,10},{10,11},{11... | collective-permute-start | bytes 122888 | tf_op jit(solution)/shard_map/ppermute | solution.py:19
  247.0 13.7 %collective-permute-start.3 = (bf16[1,8,10,1,256]{4,3,2,1,0:T(2,128)(2,1)}, bf16[1,8,10,1,256]{4,3,2,1,0:T(2,128)(2,1)}, u32[]{:S(2)}, u32[]{:S(2)}) collective-permute-start(bf16[1,8,10,1,256]{4,3,2,1,0:T(2,128)(2,1)} %get-tuple-element.26), channel_id=1, source_target_pairs={{1,0},{2,1},{3,2},{4,3},{5,4},{6,5},{7,6},{9,8},{10,9},{11,10},{12... | collective-permute-start | bytes 122888 | tf_op jit(solution)/shard_map/ppermute | solution.py:20
  260.6 8.0 copy-start.15
  261.9 6.8 copy-start.8
  268.6 9.1 %copy-start.2 = (bf16[8,10,6,1,8,33]{0,4,5,2,1,3:T(8,128)(2,1)S(1)}, bf16[8,10,6,1,8,33]{0,4,5,2,1,3:T(8,128)(2,1)}, u32[]{:S(2)}) copy-start(bf16[8,10,6,1,8,33]{0,4,5,2,1,3:T(8,128)(2,1)} %copy.347) | copy-start | bytes 760324
  268.6 9.1 %copy-start.14 = (bf16[8,16,3,3,3]{1,0,4,3,2:T(8,128)(2,1)S(1)}, bf16[8,16,3,3,3]{1,0,4,3,2:T(8,128)(2,1)}, u32[]{:S(2)}) copy-start(bf16[8,16,3,3,3]{1,0,4,3,2:T(8,128)(2,1)} %param.9) | copy-start | bytes 20740
  296.5 122.4 %collective-permute-start.12 = (bf16[1,16,1,4,256]{4,1,3,0,2:T(8,128)(2,1)}, bf16[1,16,1,4,256]{4,1,3,0,2:T(8,128)(2,1)}, u32[]{:S(2)}, u32[]{:S(2)}) collective-permute-start(bf16[1,16,1,4,256]{4,1,3,0,2:T(8,128)(2,1)} %slice_bitcast_fusion.4), channel_id=1, source_target_pairs={{0,8},{8,16},{16,24},{24,32},{32,40},{40,48},{48,56},{56,64},{64,7... | collective-permute-start | bytes 98312 | tf_op jit(solution)/shard_map/ppermute | solution.py:19
  302.9 116.1 %collective-permute-start.13 = (bf16[1,16,1,4,256]{4,1,3,0,2:T(8,128)(2,1)}, bf16[1,16,1,4,256]{4,1,3,0,2:T(8,128)(2,1)}, u32[]{:S(2)}, u32[]{:S(2)}) collective-permute-start(bf16[1,16,1,4,256]{4,1,3,0,2:T(8,128)(2,1)} %slice_bitcast_fusion.3), channel_id=1, source_target_pairs={{8,0},{16,8},{24,16},{32,24},{40,32},{48,40},{56,48},{64,56},{72,6... | collective-permute-start | bytes 98312 | tf_op jit(solution)/shard_map/ppermute | solution.py:20
  304.9 12.1 %copy-start.4 = (bf16[8,10,6,1,7,1]{5,4,2,1,0,3:T(8,128)(2,1)S(1)}, bf16[8,10,6,1,7,1]{5,4,2,1,0,3:T(8,128)(2,1)}, u32[]{:S(2)}) copy-start(bf16[8,10,6,1,7,1]{5,4,2,1,0,3:T(8,128)(2,1)} %get-tuple-element.14) | copy-start | bytes 20164
  306.4 13.5 %collective-permute-start.8 = (bf16[1,16,1,4,256]{4,1,3,0,2:T(8,128)(2,1)S(1)}, bf16[1,16,1,4,256]{4,1,3,0,2:T(8,128)(2,1)S(1)}, u32[]{:S(2)}, u32[]{:S(2)}) collective-permute-start(bf16[1,16,1,4,256]{4,1,3,0,2:T(8,128)(2,1)S(1)} %slice_bitcast_fusion.6), channel_id=1, source_target_pairs={{0,8},{8,16},{16,24},{24,32},{32,40},{40,48},{48,56},{56,64},{64,7... | collective-permute-start | bytes 98312 | tf_op jit(solution)/shard_map/ppermute | solution.py:19
  310.8 9.1 %collective-permute-start.9 = (bf16[1,16,1,4,256]{4,1,3,2,0:T(8,128)(2,1)S(1)}, bf16[1,16,1,4,256]{4,1,3,2,0:T(8,128)(2,1)S(1)}, u32[]{:S(2)}, u32[]{:S(2)}) collective-permute-start(bf16[1,16,1,4,256]{4,1,3,2,0:T(8,128)(2,1)S(1)} %slice_bitcast_fusion.5), channel_id=1, source_target_pairs={{8,0},{16,8},{24,16},{32,24},{40,32},{48,40},{56,48},{64,56},{72,6... | collective-permute-start | bytes 98312 | tf_op jit(solution)/shard_map/ppermute | solution.py:20
  319.9 16.9 %collective-permute-start.10 = (bf16[1,16,10,1,256]{4,1,3,2,0:T(8,128)(2,1)S(1)}, bf16[1,16,10,1,256]{4,1,3,2,0:T(8,128)(2,1)S(1)}, u32[]{:S(2)}, u32[]{:S(2)}) collective-permute-start(bf16[1,16,10,1,256]{4,1,3,2,0:T(8,128)(2,1)S(1)} %get-tuple-element.19), channel_id=1, source_target_pairs={{0,1},{1,2},{2,3},{3,4},{4,5},{5,6},{6,7},{8,9},{9,10},{10,11},{11... | collective-permute-start | bytes 245768 | tf_op jit(solution)/shard_map/ppermute | solution.py:19
  324.4 12.4 %collective-permute-start.11 = (bf16[1,16,10,1,256]{4,1,3,2,0:T(8,128)(2,1)S(1)}, bf16[1,16,10,1,256]{4,1,3,2,0:T(8,128)(2,1)}, u32[]{:S(2)}, u32[]{:S(2)}) collective-permute-start(bf16[1,16,10,1,256]{4,1,3,2,0:T(8,128)(2,1)S(1)} %get-tuple-element.20), channel_id=1, source_target_pairs={{1,0},{2,1},{3,2},{4,3},{5,4},{6,5},{7,6},{9,8},{10,9},{11,10},{12... | collective-permute-start | bytes 245768 | tf_op jit(solution)/shard_map/ppermute | solution.py:20
  330.3 3.5 copy-start.3
  368.1 58.1 %all-to-all-start.8 = ((f32[32,1,2048]{2,1,0:T(1,128)}), f32[32,1,2048]{2,1,0:T(1,128)S(1)}, u32[]{:S(2)}, u32[]{:S(2)}) async-start(f32[32,1,2048]{2,1,0:T(1,128)} %reshape.443), calls=%async_computation.8 | async-start | bytes 524288 | tf_op jit(solution)/shard_map/all_to_all | solution.py:47
  420.4 61.1 %collective-permute-start.14 = (bf16[1,16,10,1,256]{4,1,3,2,0:T(8,128)(2,1)}, bf16[1,16,10,1,256]{4,1,3,2,0:T(8,128)(2,1)}, u32[]{:S(2)}, u32[]{:S(2)}) collective-permute-start(bf16[1,16,10,1,256]{4,1,3,2,0:T(8,128)(2,1)} %get-tuple-element.15), channel_id=1, source_target_pairs={{0,1},{1,2},{2,3},{3,4},{4,5},{5,6},{6,7},{8,9},{9,10},{10,11},{11... | collective-permute-start | bytes 245768 | tf_op jit(solution)/shard_map/ppermute | solution.py:19
  424.3 57.2 %collective-permute-start.15 = (bf16[1,16,10,1,256]{4,1,3,2,0:T(8,128)(2,1)}, bf16[1,16,10,1,256]{4,1,3,2,0:T(8,128)(2,1)}, u32[]{:S(2)}, u32[]{:S(2)}) collective-permute-start(bf16[1,16,10,1,256]{4,1,3,2,0:T(8,128)(2,1)} %get-tuple-element.16), channel_id=1, source_target_pairs={{1,0},{2,1},{3,2},{4,3},{5,4},{6,5},{7,6},{9,8},{10,9},{11,10},{12... | collective-permute-start | bytes 245768 | tf_op jit(solution)/shard_map/ppermute | solution.py:20
  433.9 24.7 %copy-start.5 = (bf16[8,4,8,33,16]{4,2,3,1,0:T(8,128)(2,1)S(1)}, bf16[8,4,8,33,16]{4,2,3,1,0:T(8,128)(2,1)}, u32[]{:S(2)}) copy-start(bf16[8,4,8,33,16]{4,2,3,1,0:T(8,128)(2,1)} %multiply_convert_fusion) | copy-start | bytes 811012
  446.3 48.2 %all-to-all-start.9 = ((f32[32,1,2048]{2,1,0:T(1,128)}), f32[32,1,2048]{2,1,0:T(1,128)S(1)}, u32[]{:S(2)}, u32[]{:S(2)}) async-start(f32[32,1,2048]{2,1,0:T(1,128)} %reshape.445), calls=%async_computation.9 | async-start | bytes 524288 | tf_op jit(solution)/shard_map/all_to_all | solution.py:51
  498.2 347.3 %all-to-all-start.10 = ((f32[2,4,8,1024]{3,1,0,2:T(4,128)}), f32[2,4,8,1024]{3,1,0,2:T(4,128)S(1)}, u32[]{:S(2)}, u32[]{:S(2)}) async-start(f32[2,4,8,1024]{3,1,0,2:T(4,128)} %reshape.426), calls=%async_computation.10 | async-start | bytes 524288 | tf_op jit(solution)/shard_map/all_to_all | solution.py:50
  503.7 90.1 %copy-start.11 = (f32[16,8,3,3,3]{0,1,4,3,2:T(8,128)S(1)}, f32[16,8,3,3,3]{0,1,4,3,2:T(8,128)}, u32[]{:S(2)}) copy-start(f32[16,8,3,3,3]{0,1,4,3,2:T(8,128)} %fusion.52) | copy-start | bytes 41476
  503.7 342.1 %copy-start.9 = (f32[1,2,32,32]{3,2,1,0:T(8,128)S(1)}, f32[1,2,32,32]{3,2,1,0:T(8,128)}, u32[]{:S(2)}) copy-start(f32[1,2,32,32]{3,2,1,0:T(8,128)} %get-tuple-element.33) | copy-start | bytes 24580
  503.7 342.1 %copy-start.10 = (f32[1,2,32,32]{3,2,1,0:T(8,128)S(1)}, f32[1,2,32,32]{3,2,1,0:T(8,128)}, u32[]{:S(2)}) copy-start(f32[1,2,32,32]{3,2,1,0:T(8,128)} %get-tuple-element.34) | copy-start | bytes 24580
  860.5 13.3 %all-to-all-start.11 = ((bf16[8,2,4096]{2,1,0:T(2,128)(2,1)}), bf16[8,2,4096]{2,1,0:T(2,128)(2,1)S(1)}, u32[]{:S(2)}, u32[]{:S(2)}) async-start(bf16[8,2,4096]{2,1,0:T(2,128)(2,1)} %reshape.447), calls=%async_computation.11 | async-start | bytes 262144 | tf_op jit(solution)/shard_map/all_to_all | solution.py:62
  867.9 26.4 %copy-start.1 = (bf16[16,8,3,3,3]{0,1,4,3,2:T(8,128)(2,1)S(1)}, bf16[16,8,3,3,3]{0,1,4,3,2:T(8,128)(2,1)}, u32[]{:S(2)}) copy-start(bf16[16,8,3,3,3]{0,1,4,3,2:T(8,128)(2,1)} %param.8) | copy-start | bytes 20740
  868.6 24.8 %copy-start.7 = (f32[2,4,8,4,256]{4,3,2,1,0:T(4,128)S(1)}, f32[2,4,8,4,256]{4,3,2,1,0:T(4,128)}, u32[]{:S(2)}) copy-start(f32[2,4,8,4,256]{4,3,2,1,0:T(4,128)} %param.7) | copy-start | bytes 786436
  868.6 24.9 %copy-start.12 = (f32[8,4]{1,0:T(8,128)S(1)}, f32[8,4]{1,0:T(8,128)}, u32[]{:S(2)}) copy-start(f32[8,4]{1,0:T(8,128)} %copy.333) | copy-start | bytes 388
